TPU v7x, 32 devices: a whole 2x2x4 slice. The times are simulated.
32 devices in a mesh: row: 4 (over x, core), col: 8 (over z, y).
Axes of the slice: x: 2, y: 2, z: 4, core: 2. Of those that a mesh axis runs over, the one named last changes fastest.
Arguments:
- diag_coords: int32 [2, 1536], replicated, may hold values from 0 to 32767
- panel_coords: int32 [2, 8, 1536], P(None, 'row', 'col'), may hold values from 0 to 32767
- test_matrix: bfloat16 [8, 1536, 512], P('row', 'col'), may hold values from -6 to 6
- ranks: int32 [8], replicated, may hold values from 64 to 512, as said below
Outputs:
- panel_left: bfloat16 [8, 1536, 512], P('row', 'col')
- update_right: bfloat16 [8, 8, 1536, 512], P('row', 'col')
Inputs may be any that keep to these rules, and one draw needn't show every extreme that they name: ranks[i] is 512 at tile 0 and 64 at the last tile and falls roughly evenly in between, with small random steps.
All inputs are finite; a program needn't handle non-finite values.
Results may differ from a plain program's by a relative error of at most 0.0068.
Values may be sent and summed in bfloat16 or wider, within the bound.
A program may use at most 256 MiB of HBM per device.

v0:
```python
import jax
import jax.numpy as jnp
from jax import lax
from jax.sharding import PartitionSpec as P

range_length = 409.6
nugget = 0.5
shift_ratio = 0.01


def broadcast(value, axis, root):
    mine = lax.axis_index(axis) == root
    return lax.psum(jnp.where(mine, value, jnp.zeros_like(value)), axis)


def matern(first, second):
    delta_x = (first[0][:, None] - second[0][None, :]).astype(jnp.float32)
    delta_y = (first[1][:, None] - second[1][None, :]).astype(jnp.float32)
    return jnp.exp(-jnp.sqrt(delta_x * delta_x + delta_y * delta_y) / range_length)


def solve_right(factor, sample):
    return jax.scipy.linalg.solve_triangular(factor, sample.T, lower=True).T


def shards(diag_coords, panel_coords, test_matrix, ranks):
    points = diag_coords.shape[1]
    row_tiles = panel_coords.shape[1]
    width = test_matrix.shape[2]
    n_row = lax.axis_size("row")
    n_col = lax.axis_size("col")
    col_tiles = row_tiles * n_row // n_col
    row_index = lax.axis_index("row")
    col_index = lax.axis_index("col")
    cov = matern(diag_coords, diag_coords) + nugget * jnp.eye(points, dtype=jnp.float32)
    is_owner = (row_index == 0) & (col_index == 0)
    lower = lax.cond(is_owner, jnp.linalg.cholesky, jnp.zeros_like, cov)
    lower = broadcast(lower, ("row", "col"), 0)
    columns = jnp.arange(width, dtype=jnp.int32)
    row_ranks = lax.dynamic_slice_in_dim(ranks, row_index * row_tiles, row_tiles)
    row_mask = (columns[None, :] < row_ranks[:, None]).astype(jnp.float32)
    tests_full = lax.all_gather(test_matrix, "col", axis=1, tiled=True)
    tests_rows = tests_full * row_mask.astype(jnp.bfloat16)[:, None, :]
    local_points = panel_coords.reshape(2, -1)
    block = matern(local_points, diag_coords)
    solved = jax.scipy.linalg.solve_triangular(lower, block.T, lower=True).T
    solved = solved.reshape(row_tiles, -1, points)
    sample = jnp.einsum(
        "inm,imr->inr", solved, tests_rows.astype(jnp.float32), precision=lax.Precision.HIGHEST
    )
    gram_part = jnp.einsum("inr,ins->irs", sample, sample, precision=lax.Precision.HIGHEST)
    gram = lax.psum(gram_part, "col")
    trace = jnp.sum(jnp.diagonal(gram, axis1=1, axis2=2), axis=1)
    shift = shift_ratio * trace / row_ranks.astype(jnp.float32)
    extra = shift[:, None] * row_mask + 1.0 - row_mask
    shifted = gram + extra[:, :, None] * jnp.eye(width, dtype=jnp.float32)[None]
    factor = jnp.linalg.cholesky(shifted)
    left = jax.vmap(solve_right)(factor, sample).astype(jnp.bfloat16)
    coeff_part = jnp.einsum(
        "inm,inr->imr", solved, left.astype(jnp.float32), precision=lax.Precision.HIGHEST
    )
    coeff_piece = lax.psum_scatter(coeff_part, "col", scatter_dimension=1, tiled=True).astype(
        jnp.bfloat16
    )
    coeff = lax.all_gather(coeff_piece, "col", axis=1, tiled=True)
    left_full = lax.all_gather(left, "col", axis=1, tiled=True)
    root = col_index * col_tiles // row_tiles
    stacked = jnp.stack([left_full, coeff])
    slab = broadcast(stacked, "row", root)
    offset = col_index * col_tiles % row_tiles
    col_left = lax.dynamic_slice_in_dim(slab[0], offset, col_tiles, 0)
    col_coeff = lax.dynamic_slice_in_dim(slab[1], offset, col_tiles, 0)
    core = jnp.einsum("inr,jns->ijrs", coeff, col_coeff, preferred_element_type=jnp.float32)
    core = core.astype(jnp.bfloat16)
    update = jnp.einsum("jns,ijrs->ijnr", col_left, core, preferred_element_type=jnp.float32)
    return (left, update.astype(jnp.bfloat16))


def solution(mesh):
    in_specs = (P(), P(None, "row", "col"), P("row", "col", None), P())
    out_specs = (P("row", "col", None), P("row", "col", None, None))
    return jax.shard_map(shards, mesh=mesh, in_specs=in_specs, out_specs=out_specs, check_vma=False)
```

profile of v0, /device:TPU:0, one launch (start us, length us, event | category | flops | bytes accessed | tf_op | source)
XLA Modules:
  0.0 1702.9 jit_solution(14730289430506334568)
XLA Ops:
  29.8 378.8 %conditional.1 = (f32[1536,1536]{1,0:T(8,128)}) conditional(s32[]{:T(128)} %convert_element_type.73, () %tuple.15, (f32[1536,1536]{1,0:T(8,128)}, f32[1536,1536]{1,0:T(8,128)}, s32[1536,1536]{1,0:T(8,128)}, s32[1536,1536]{1,0:T(8,128)}, f32[1536,1536]{1,0:T(8,128)}) %tuple.16), branch_computations={%region_0.0_spmd, %region_1.26_spmd} | conditional | flops 8891072512 | bytes 176959488 | solution.py:37
  29.8 20.5 %select_add_fusion = f32[1536,1536]{1,0:T(8,128)} fusion(f32[1536,1536]{1,0:T(8,128)} %get-tuple-element.31, f32[1536,1536]{1,0:T(8,128)} %get-tuple-element.28, f32[1536,1536]{1,0:T(8,128)} %get-tuple-element.27, s32[1536,1536]{1,0:T(8,128)} %get-tuple-element.29, s32[1536,1536]{1,0:T(8,128)} %get-tuple-element.30), kind=kLoop, calls=%fused_computation.4 | loop fusion | flops 18874368 | bytes 56623104 | tf_op jit(solution)/shard_map/add | solution.py:35
  60.0 12.2 fusion
  103.9 11.9 cholesky.28
  132.6 11.7 cholesky.55
  161.3 11.7 cholesky.80
  189.7 11.9 cholesky.109
  218.5 11.7 cholesky.139
  247.2 11.7 cholesky.169
  276.1 11.7 cholesky.199
  304.3 11.9 cholesky.229
  332.2 11.7 cholesky.259
  359.6 11.7 cholesky.289
  386.1 11.7 cholesky.317
  419.4 216.4 %all-reduce.6.cloned.1.call-done = f32[1536,1536]{1,0:T(8,128)} async-done(((f32[1536,1536]{1,0:T(8,128)}), f32[1536,1536]{1,0:T(8,128)}) %all-reduce.6.cloned.1.call-update) | async-done | bytes 9437200 | tf_op jit(solution)/shard_map/psum | solution.py:13
  644.2 43.1 %while.2 = (s32[]{:T(128)}, f32[1536,1536]{1,0:T(8,128)}, s32[12,2]{0,1:T(2,128)S(1)}, f32[12,128,128]{2,1,0:T(8,128)}, s32[]{:T(128)}) while((s32[]{:T(128)}, f32[1536,1536]{1,0:T(8,128)}, s32[12,2]{0,1:T(2,128)S(1)}, f32[12,128,128]{2,1,0:T(8,128)}, s32[]{:T(128)}) %tuple.147), condition=%wide.while_cond, body=%wide.while_body.sunk | while | flops 2 | bytes 132705 | solution.py:46
  687.2 118.8 %custom-call.130 = f32[12,128,128]{1,2,0:T(8,128)S(1)} custom-call(f32[12,128,128]{2,1,0:T(8,128)} %get-tuple-element.41), custom_call_target="InvertDiagBlocksLowerTriangular" | custom-call | tf_op jit(solution)/shard_map/jit(_solve_triangular)/triangular_solve | solution.py:46
  845.9 99.9 %all-reduce.8.cloned.1.call-done = f32[2,512,512]{1,2,0:T(8,128)} async-done(((f32[2,512,512]{1,2,0:T(8,128)}), f32[2,512,512]{1,2,0:T(8,128)}) %all-reduce.8.cloned.1.call-update) | async-done | bytes 2097168 | tf_op jit(solution)/shard_map/psum | solution.py:52
  945.7 60.5 %copy.47 = f32[2,512,512]{0,2,1:T(8,128)} copy(f32[2,512,512]{1,2,0:T(8,128)} %all-reduce.8.cloned.1.call-done) | data formatting | bytes 4194304 | tf_op jit(solution)/shard_map/psum | solution.py:52
  1023.1 23.5 %custom-call.131 = f32[2,128,128]{2,1,0:T(8,128)S(1)} custom-call(f32[2,128,128]{2,1,0:T(8,128)S(1)} %cholesky.986), custom_call_target="Cholesky" | custom-call | tf_op jit(solution)/shard_map/jit(cholesky)/cholesky | solution.py:57
  1048.8 20.5 %custom-call.132 = f32[2,1,128,128]{2,3,1,0:T(8,128)S(1)} custom-call(f32[2,1,128,128]{3,2,1,0:T(8,128)} %select_bitcast_fusion.13), custom_call_target="InvertDiagBlocksLowerTriangular" | custom-call | tf_op jit(solution)/shard_map/jit(cholesky)/cholesky | solution.py:57
  1073.7 25.0 %custom-call.133 = f32[2,128,128]{2,1,0:T(8,128)} custom-call(f32[2,128,128]{2,1,0:T(8,128)} %cholesky.990), custom_call_target="Cholesky" | custom-call | tf_op jit(solution)/shard_map/jit(cholesky)/cholesky | solution.py:57
  1100.3 21.1 %custom-call.134 = f32[2,1,128,128]{2,3,1,0:T(8,128)} custom-call(f32[2,1,128,128]{3,2,1,0:T(8,128)} %get-tuple-element.192), custom_call_target="InvertDiagBlocksLowerTriangular" | custom-call | tf_op jit(solution)/shard_map/jit(cholesky)/cholesky | solution.py:57
  1125.9 24.9 %custom-call.135 = f32[2,128,128]{2,1,0:T(8,128)} custom-call(f32[2,128,128]{2,1,0:T(8,128)} %cholesky.995), custom_call_target="Cholesky" | custom-call | tf_op jit(solution)/shard_map/jit(cholesky)/cholesky | solution.py:57
  1152.4 21.3 %custom-call.136 = f32[2,1,128,128]{2,3,1,0:T(8,128)} custom-call(f32[2,1,128,128]{3,2,1,0:T(8,128)} %get-tuple-element.190), custom_call_target="InvertDiagBlocksLowerTriangular" | custom-call | tf_op jit(solution)/shard_map/jit(cholesky)/cholesky | solution.py:57
  1177.3 23.5 %custom-call.137 = f32[2,128,128]{2,1,0:T(8,128)S(1)} custom-call(f32[2,128,128]{2,1,0:T(8,128)S(1)} %convolution_subtract_fusion.20), custom_call_target="Cholesky" | custom-call | tf_op jit(solution)/shard_map/jit(cholesky)/cholesky | solution.py:57
  1206.3 14.4 while.3
  1220.8 80.3 %custom-call.138 = f32[2,4,128,128]{2,3,1,0:T(8,128)} custom-call(f32[2,4,128,128]{3,2,1,0:T(8,128)} %bitcast.263), custom_call_target="InvertDiagBlocksLowerTriangular" | custom-call | tf_op jit(solution)/shard_map/vmap(jit(_solve_triangular))/triangular_solve | solution.py:23
  1314.5 115.9 %reduce-scatter.2.cloned.1.call-done = f32[2,192,512]{2,1,0:T(8,128)} async-done(((f32[2,1536,512]{2,1,0:T(8,128)}), f32[2,192,512]{2,1,0:T(8,128)}) %reduce-scatter.2.cloned.1.call-update) | async-done | bytes 786448 | tf_op jit(solution)/shard_map/reduce_scatter | solution.py:62
  1432.5 60.6 %all-gather.6.cloned.1.call-done = bf16[2,1536,512]{2,1,0:T(8,128)(2,1)} async-done(((bf16[2,192,512]{2,1,0:T(8,128)(2,1)}), bf16[2,1536,512]{2,1,0:T(8,128)(2,1)}) %all-gather.6.cloned.1.call-update) | async-done | bytes 3145744 | tf_op jit(solution)/shard_map/all_gather | solution.py:66
  1493.1 62.0 %all-gather.8.cloned.1.call-done = bf16[2,1536,512]{2,1,0:T(8,128)(2,1)} async-done(((bf16[2,192,512]{2,1,0:T(8,128)(2,1)}), bf16[2,1536,512]{2,1,0:T(8,128)(2,1)}) %all-gather.8.cloned.1.call-update) | async-done | bytes 3145744 | tf_op jit(solution)/shard_map/all_gather | solution.py:65
  1561.6 118.4 %all-reduce.10.cloned.1.call-done = bf16[2,2,1536,512]{3,2,1,0:T(8,128)(2,1)} async-done(((bf16[2,2,1536,512]{3,2,1,0:T(8,128)(2,1)}), bf16[2,2,1536,512]{3,2,1,0:T(8,128)(2,1)}) %all-reduce.10.cloned.1.call-update) | async-done | bytes 6291472 | tf_op jit(solution)/shard_map/psum | solution.py:13
  (241 shorter events, 423.4 us)
Async XLA Ops:
  8.0 627.8 %all-reduce.6.cloned.1.call-start = ((), (), s32[]{:S(2)}) async-start(), calls=%async_computation.1 | async-start | bytes 18874368 | tf_op jit(solution)/shard_map/psum | solution.py:13
  417.0 0.7 copy-start.6
  417.0 0.9 copy-start.7
  417.0 419.0 %all-gather.4.cloned.1.call-start = ((), (), s32[]{:S(2)}) async-start(), calls=%async_computation.2 | async-start | bytes 3538944 | tf_op jit(solution)/shard_map/all_gather | solution.py:42
  417.6 528.1 %all-reduce.8.cloned.1.call-start = ((), (), s32[]{:S(2)}) async-start(), calls=%async_computation.3 | async-start | bytes 4194304 | tf_op jit(solution)/shard_map/psum | solution.py:52
  832.5 1.4 copy-start.1
  843.3 587.2 %reduce-scatter.2.cloned.1.call-start = ((), (), s32[]{:S(2)}) async-start(), calls=%async_computation.5 | async-start | bytes 7077888 | tf_op jit(solution)/shard_map/reduce_scatter | solution.py:62
  843.4 204.8 %copy-start.5 = (pred[128,128]{1,0:T(8,128)(4,1)}, pred[128,128]{1,0:T(8,128)(4,1)S(1)}, u32[]{:S(2)}) copy-start(pred[128,128]{1,0:T(8,128)(4,1)S(1)} %iota_compare_fusion.6) | copy-start | bytes 49156
  1021.7 1.4 copy-start
  1046.5 25.0 %copy-start.2 = (f32[2,128,128]{2,1,0:T(8,128)}, f32[2,128,128]{2,1,0:T(8,128)S(1)}, u32[]{:S(2)}) copy-start(f32[2,128,128]{2,1,0:T(8,128)S(1)} %custom-call.131) | copy-start | bytes 393220
  1123.4 77.4 %copy-start.3 = (f32[2,128,128]{2,1,0:T(8,128)S(1)}, f32[2,128,128]{2,1,0:T(8,128)}, u32[]{:S(2)}) copy-start(f32[2,128,128]{2,1,0:T(8,128)} %copy-done.2) | copy-start | bytes 393220
  1301.0 5.3 copy-start.4
  1313.6 179.4 %all-gather.6.cloned.1.call-start = ((), (), s32[]{:S(2)}) async-start(), calls=%async_computation.4 | async-start | bytes 3538944 | tf_op jit(solution)/shard_map/all_gather | solution.py:66
  1314.5 240.6 %all-gather.8.cloned.1.call-start = ((), (), s32[]{:S(2)}) async-start(), calls=%async_computation.6 | async-start | bytes 3538944 | tf_op jit(solution)/shard_map/all_gather | solution.py:65
  1432.4 247.5 %all-reduce.10.cloned.1.call-start = ((), (), s32[]{:S(2)}) async-start(), calls=%async_computation.7 | async-start | bytes 12582912 | tf_op jit(solution)/shard_map/psum | solution.py:13
Sparse Core Ops, SparseCore 0:
  417.1 218.6 all-reduce.5
  1561.7 118.2 all-reduce.9
Sparse Core Ops, SparseCore 1:
  419.9 84.1 all-gather.3
  843.3 102.3 all-reduce.7
  1313.7 116.7 reduce-scatter.1
  1433.5 59.5 all-gather.5
  1496.1 58.9 all-gather.7
where the time goes:
time: 1710 us; the launch traced here: 1700 us
  other arithmetic  717 us (42%)
  waiting for transfers between devices  674 us (39%)
  local copies, waits for them, and re-layouts  173 us (10%)
  matrix products  114 us (7%)
    psum x2, waiting for transfers between devices, broadcast(): return lax.psum(jnp.where(mine, value, jnp.zeros_like(value)), axis)  335 us
    another operation x46, other arithmetic, shards(): lower = lax.cond(is_owner, jnp.linalg.cholesky, jnp.zeros_like, cov)  264 us
    another operation x18, other arithmetic, shards(): factor = jnp.linalg.cholesky(shifted)  166 us
    another operation x3, other arithmetic, shards(): solved = jax.scipy.linalg.solve_triangular(lower, block.T, lower=True).T  127 us
    reduce_scatter x1, waiting for transfers between devices, shards(): lax.psum_scatter(coeff_part, 'col', scatter_dimension=1, tiled=True)  116 us
    psum x1, waiting for transfers between devices, shards(): gram = lax.psum(gram_part, 'col')  99.9 us
    another operation x4, other arithmetic, solve_right(): return jax.scipy.linalg.solve_triangular(factor, sample.T, lower=True).T  84.4 us
    another operation x49, local copies, waits for them, and re-layouts  62.3 us
  transfers between devices with their start and end apart: 7, of which 6 were waited for; matrix products, arithmetic and copies ran while one was open for 12% of the time, Pallas kernels for 0%

commit v1 on v0

v1 whole, which is shorter than its diff:
```python
import functools

import jax
import jax.numpy as jnp
from jax import lax
from jax.experimental import pallas as pl
from jax.experimental.pallas import tpu as pltpu
from jax.sharding import PartitionSpec as P

range_length = 409.6
nugget = 0.5
shift_ratio = 0.01
BLOCK = 128
SUB = 8


def matern(first, second):
    delta_x = (first[0][:, None] - second[0][None, :]).astype(jnp.float32)
    delta_y = (first[1][:, None] - second[1][None, :]).astype(jnp.float32)
    return jnp.exp(-jnp.sqrt(delta_x * delta_x + delta_y * delta_y) / range_length)


def split(value):
    high = value.astype(jnp.bfloat16)
    low = (value - high.astype(jnp.float32)).astype(jnp.bfloat16)
    return high, low


def contract_rows(first, second):
    return lax.dot_general(first, second, (((0,), (0,)), ((), ())), preferred_element_type=jnp.float32)


def leaf(work):
    lane = lax.broadcasted_iota(jnp.int32, (SUB, BLOCK), 1)
    sub = lax.broadcasted_iota(jnp.int32, (SUB, BLOCK), 0)
    for panel in range(BLOCK // SUB):
        start = panel * SUB
        end = start + SUB
        rows = work[start:end, :]
        columns = [jnp.broadcast_to(rows[:, start + j : start + j + 1], (SUB, BLOCK)) for j in range(SUB)]
        inside = (lane >= start) & (lane < end)
        rows = jnp.where(inside, (lane - start == sub).astype(jnp.float32), rows)
        pivots = jnp.ones((SUB, BLOCK), jnp.float32)
        for k in range(SUB):
            pivot = jnp.broadcast_to(columns[k][k : k + 1, :], (SUB, BLOCK))
            pivots = jnp.where(sub == k, pivot, pivots)
            if k == SUB - 1:
                break
            factor = jnp.where(sub > k, columns[k] * (1.0 / pivot), 0.0)
            rows = rows - factor * rows[k : k + 1, :]
            for j in range(k + 1, SUB):
                columns[j] = columns[j] - factor * columns[j][k : k + 1, :]
        rows = rows * lax.rsqrt(pivots)
        work[start:end, :] = rows
        if end < BLOCK:
            right = jnp.where(lane >= end, rows, 0.0)
            change = lax.dot_general(
                right, rows, (((0,), (0,)), ((), ())),
                precision=lax.Precision.HIGHEST, preferred_element_type=jnp.float32,
            )
            below = work[end:, :]
            lanes = lax.broadcasted_iota(jnp.int32, below.shape, 1)
            below = jnp.where((lanes >= start) & (lanes < end), 0.0, below)
            work[end:, :] = below - change[end:, :]


def factor_kernel(a_ref, out_ref, work, left, right):
    size = a_ref.shape[0]
    blocks = size // BLOCK

    @pl.loop(0, blocks)
    def _(i):
        at = pl.ds(pl.multiple_of(i * BLOCK, BLOCK), BLOCK)
        out_ref[at, :] = a_ref[at, :]

    @pl.loop(0, blocks)
    def _(k):
        start = pl.multiple_of(k * BLOCK, BLOCK)
        at = pl.ds(start, BLOCK)
        work[...] = out_ref[at, at]
        leaf(work)
        row = lax.broadcasted_iota(jnp.int32, (BLOCK, BLOCK), 0)
        col = lax.broadcasted_iota(jnp.int32, (BLOCK, BLOCK), 1)
        inverse = jnp.where(row >= col, work[...], 0.0)
        high, low = split(inverse)
        both = jnp.concatenate([high, high, low], axis=1)
        p_high, p_low = split(out_ref[at, :])
        stacked = jnp.concatenate([p_high, p_low, p_high], axis=0)
        panel = jnp.dot(both, stacked, preferred_element_type=jnp.float32)
        wide = lax.broadcasted_iota(jnp.int32, (BLOCK, size), 1)
        out_ref[at, :] = jnp.where(wide < start, panel, 0.0)
        out_ref[at, at] = inverse
        r_high, r_low = split(panel)
        left[0:BLOCK, :] = r_high
        left[BLOCK : 2 * BLOCK, :] = r_high
        left[2 * BLOCK :, :] = r_low
        right[0:BLOCK, :] = r_high
        right[BLOCK : 2 * BLOCK, :] = r_low
        right[2 * BLOCK :, :] = r_high
        right[0:BLOCK, at] = high
        right[BLOCK : 2 * BLOCK, at] = low
        right[2 * BLOCK :, at] = high

        @pl.loop(k + 1, blocks)
        def _(i):
            rows = pl.ds(pl.multiple_of(i * BLOCK, BLOCK), BLOCK)
            out_ref[rows, at] = jnp.zeros((BLOCK, BLOCK), jnp.float32)
            out_ref[rows, :] = out_ref[rows, :] - contract_rows(left[:, rows], right[...])


def inverse_factor(matrix):
    size = matrix.shape[0]
    return pl.pallas_call(
        factor_kernel,
        out_shape=jax.ShapeDtypeStruct((size, size), jnp.float32),
        in_specs=[pl.BlockSpec(memory_space=pltpu.VMEM)],
        out_specs=pl.BlockSpec(memory_space=pltpu.VMEM),
        scratch_shapes=[
            pltpu.VMEM((BLOCK, BLOCK), jnp.float32),
            pltpu.VMEM((3 * BLOCK, size), jnp.bfloat16),
            pltpu.VMEM((3 * BLOCK, size), jnp.bfloat16),
        ],
        compiler_params=pltpu.CompilerParams(vmem_limit_bytes=48 * 1024 * 1024),
        cost_estimate=pl.CostEstimate(
            flops=size * 400000 + 6 * size**3, bytes_accessed=8 * size * size, transcendentals=0
        ),
    )(matrix)


def high_dot(spec, first, second):
    return jnp.einsum(spec, first, second, precision=lax.Precision.HIGH, preferred_element_type=jnp.float32)


def spread(value, n_row, n_col, row_tiles, row_index, col_index):
    root = col_index // row_tiles
    reached = n_row
    step = n_row // 2
    while step >= 1:
        pairs = []
        for b in range(n_col):
            source = b // row_tiles
            for a in range(n_row):
                if (a ^ source) % reached == 0:
                    pairs.append((a * n_col + b, (a ^ step) * n_col + b))
        moved = lax.ppermute(value, ("row", "col"), pairs)
        gets = ((row_index ^ root) % reached) == step
        value = jnp.where(gets, moved, value)
        reached = step
        step //= 2
    return value


def shards(diag_coords, panel_coords, test_matrix, ranks):
    points = diag_coords.shape[1]
    row_tiles = panel_coords.shape[1]
    width = test_matrix.shape[2]
    share = test_matrix.shape[1]
    n_row = lax.axis_size("row")
    n_col = lax.axis_size("col")
    row_index = lax.axis_index("row")
    col_index = lax.axis_index("col")
    own = col_index % row_tiles
    tile = row_index * row_tiles + own

    all_points = lax.all_gather(panel_coords, "col", axis=2, tiled=True)
    all_tests = lax.all_gather(test_matrix, "col", axis=1, tiled=True)
    cov = matern(diag_coords, diag_coords) + nugget * jnp.eye(points, dtype=jnp.float32)
    lower_inverse = inverse_factor(cov)

    columns = jnp.arange(width, dtype=jnp.int32)
    rank = lax.dynamic_index_in_dim(ranks, tile, 0, keepdims=False)
    mask = (columns < rank).astype(jnp.float32)
    tests = lax.dynamic_index_in_dim(all_tests, own, 0, keepdims=False)
    tests = tests * mask.astype(jnp.bfloat16)[None, :]
    tile_points = lax.dynamic_index_in_dim(all_points, own, 1, keepdims=False)
    block = matern(tile_points, diag_coords)

    weights = high_dot("mk,mr->kr", lower_inverse, tests.astype(jnp.float32))
    sample = high_dot("nk,kr->nr", block, weights)
    gram = high_dot("nr,ns->rs", sample, sample)
    shift = shift_ratio * jnp.trace(gram) / rank.astype(jnp.float32)
    shifted = gram + jnp.diag(shift * mask + 1.0 - mask)
    factor_inverse = inverse_factor(shifted)
    basis = high_dot("nr,sr->ns", sample, factor_inverse).astype(jnp.bfloat16)
    projected = high_dot("nm,nr->mr", block, basis.astype(jnp.float32))
    coeff = high_dot("km,mr->kr", lower_inverse, projected).astype(jnp.bfloat16)

    both = spread(jnp.stack([basis, coeff]), n_row, n_col, row_tiles, row_index, col_index)
    pieces = basis.reshape(n_col, share, width)
    lefts, coeffs = [], []
    for step in range(row_tiles):
        if step == 0:
            lefts.append(lax.dynamic_index_in_dim(pieces, col_index, 0, keepdims=False))
            coeffs.append(coeff)
            continue
        target = [b // row_tiles * row_tiles + (b - step) % row_tiles for b in range(n_col)]
        pairs = [(b, target[b]) for b in range(n_col)]
        to = col_index // row_tiles * row_tiles + (col_index - step) % row_tiles
        coeffs.append(lax.ppermute(coeff, "col", pairs))
        lefts.append(lax.ppermute(lax.dynamic_index_in_dim(pieces, to, 0, keepdims=False), "col", pairs))
    def ordered(entries):
        stack = jnp.stack(entries)
        return jnp.roll(stack, own, axis=0) if row_tiles > 1 else stack

    left = ordered(lefts)
    row_coeff = ordered(coeffs)
    col_left, col_coeff = both[0], both[1]
    core = jnp.einsum("inr,ns->irs", row_coeff, col_coeff, preferred_element_type=jnp.float32)
    core = core.astype(jnp.bfloat16)
    update = jnp.einsum("ns,irs->inr", col_left, core, preferred_element_type=jnp.float32)
    return (left, update.astype(jnp.bfloat16)[:, None])


def solution(mesh):
    in_specs = (P(), P(None, "row", "col"), P("row", "col", None), P())
    out_specs = (P("row", "col", None), P("row", "col", None, None))
    return jax.shard_map(shards, mesh=mesh, in_specs=in_specs, out_specs=out_specs, check_vma=False)
```

time: 1710 us -> 427 us (0.25)
  other arithmetic: 717 us -> 18.6 us
  waiting for transfers between devices: 674 us -> 54.6 us
  Pallas kernels: 0 us -> 161 us
  local copies, waits for them, and re-layouts: 173 us -> 66.6 us
  matrix products: 114 us -> 53 us
  blocking collectives: 0 us -> 44.5 us
    another operation x71 -> x1, other arithmetic: 642 us -> 1.94 us  [shards(): jnp.stack([basis, coeff])]
    psum x3 -> x0, waiting for transfers between devices: 435 us -> none  [the longest x2 335 us: broadcast(): return lax.psum(jnp.where(mine, value, jnp.zeros_like(value)), axis)]
    pallas_call x0 -> x2, Pallas kernels: none -> 161 us  [inverse_factor(): pl.pallas_call(factor_kernel, out_shape=jax.ShapeDtypeStruct((size, size)...]
    all_gather x3 -> x1, waiting for transfers between devices: 123 us -> 0.01 us  [shards(): all_tests = lax.all_gather(test_matrix, 'col', axis=1, tiled=True)]
    reduce_scatter x1 -> x0, waiting for transfers between devices: 116 us -> none  [shards(): lax.psum_scatter(coeff_part, 'col', scatter_dimension=1, tiled=True)]
    another operation x58 -> x0, matrix products: 95.2 us -> none  [the longest x22 50.1 us: shards(): lower = lax.cond(is_owner, jnp.linalg.cholesky, jnp.zeros_like, cov)]
    another operation x68 -> x0, local copies, waits for them, and re-layouts: 75.6 us -> none
    psum x1 -> x0, local copies, waits for them, and re-layouts: 60.5 us -> none  [shards(): gram = lax.psum(gram_part, 'col')]
  transfers between devices with their start and end apart: 7 -> 5, of which waited for: 6 -> 2; matrix products, arithmetic and copies ran while one was open for 12% -> 18% of each run, Pallas kernels for 0% -> 30%
where the time goes in v1:
time: 427 us; the launch traced here: 424 us
  Pallas kernels  161 us (38%)
  local copies, waits for them, and re-layouts  66.6 us (16%)
  waiting for transfers between devices  54.6 us (13%)
  matrix products  53 us (12%)
  blocking collectives  44.5 us (10%)
  other arithmetic  18.6 us (4%)
  between operations  15.8 us (4%)
  starting transfers between devices  9.87 us (2%)
    pallas_call x2, Pallas kernels, inverse_factor(): pl.pallas_call(factor_kernel, out_shape=jax.ShapeDtypeStruct((size, size)...  161 us
    slice x2, local copies, waits for them, and re-layouts, matern(): delta_x = (first[0][:, None] - second[0][None, :]).astype(jnp.float32)  59.8 us
    all_gather x1, blocking collectives, shards(): all_points = lax.all_gather(panel_coords, 'col', axis=2, tiled=True)  44.5 us
    dot_general x6, matrix products, high_dot(): jnp.einsum(spec, first, second, precision=lax.Precision.HIGH, preferred_e...  43.7 us
    ppermute x2, waiting for transfers between devices, spread(): moved = lax.ppermute(value, ('row', 'col'), pairs)  33.4 us
    ppermute x1, waiting for transfers between devices, shards(): lax.ppermute(lax.dynamic_index_in_dim(pieces, to, 0, keepdims=False), 'co...  20.5 us
    dot_general x1, matrix products, shards(): jnp.einsum('ns,irs->inr', col_left, core, preferred_element_type=jnp.floa...  9.29 us
    add x1, other arithmetic, shards(): matern(diag_coords, diag_coords)  8.85 us
  transfers between devices with their start and end apart: 5, of which 2 were waited for; matrix products, arithmetic and copies ran while one was open for 18% of the time, Pallas kernels for 30%

profile of v1, /device:TPU:0, one launch (start us, length us, event | category | flops | bytes accessed | tf_op | source)
XLA Modules:
  0.0 423.6 jit_solution(16463427741168435572)
XLA Ops:
  7.2 0.0 all-gather.2.cloned.1.call-start
  7.2 0.7 all-gather.2.cloned.1.call-update
  7.9 0.8 copy.9
  8.8 1.2 dynamic_slice.29
  10.7 44.5 %all_gather.6 = s32[2,2,1536]{1,0,2:T(2,128)S(1)} all-gather(s32[2,2,192]{1,0,2:T(2,128)S(1)} %copy.9), channel_id=1, replica_groups=mesh['row'=4,'col'=8] {'col'}, dimensions={2}, use_global_device_ids=true | all-gather | bytes 27648 | tf_op jit(solution)/shard_map/all_gather | solution.py:165
  55.1 0.6 convert_convert_fusion
  55.8 0.8 slice_reduce_fusion.1
  56.6 59.0 %dynamic-slice_reduce_fusion.1 = (s32[1536]{0:T(1024)S(1)}, s32[1536]{0:T(1024)S(1)}) fusion(s32[2,2,1536]{1,0,2:T(2,128)S(1)} %all_gather.6, s32[]{:T(128)S(6)} %select_n.84, s32[]{:T(128)S(6)} %add.96), kind=kLoop, calls=%fused_computation.40 | loop fusion | bytes 24584 | tf_op jit(solution)/shard_map/slice | solution.py:18
  115.6 8.8 %select_add_fusion.a_ref = f32[1536,1536]{1,0:T(8,128)} fusion(s32[1536]{0:T(1024)S(1)} %get-tuple-element.11, s32[1536]{0:T(1024)S(1)} %get-tuple-element.10), kind=kLoop, calls=%fused_computation | loop fusion | flops 28311552 | bytes 9449472 | tf_op jit(solution)/shard_map/add | solution.py:167
  124.5 128.5 %shard_map.59 = f32[1536,1536]{1,0:T(8,128)} custom-call(f32[1536,1536]{1,0:T(8,128)} %select_add_fusion.a_ref), custom_call_target="tpu_custom_call" | custom-call | flops 22357671936 | bytes 18874368 | tf_op jit(solution)/shard_map/pallas_call | solution.py:113
  253.0 8.3 %fusion.18 = f32[1536,512]{1,0:T(8,128)S(1)} fusion(f32[1536,1536]{1,0:T(8,128)} %shard_map.59, bf16[2,1536,512]{2,1,0:T(8,128)(2,1)} %all-gather.2.cloned.1.call-done, s32[]{:T(128)S(6)} %select_n.84, bf16[512]{0:T(512)(128)(2,1)S(1)} %convert_convert_fusion), kind=kOutput, calls=%fused_computation.33 | convolution fusion | flops 7248543744 | bytes 14156804 | tf_op jit(solution)/shard_map/mk,mr->kr/dot_general | solution.py:131
  261.3 11.8 %fusion.1 = f32[1536,512]{1,0:T(8,128)S(1)} fusion(f32[1536,512]{1,0:T(8,128)S(1)} %fusion.18, s32[1536]{0:T(1024)S(1)} %get-tuple-element.11, s32[1536]{0:T(1024)S(1)} %get-tuple-element.9, s32[1536]{0:T(1024)S(1)} %get-tuple-element.10, s32[1536]{0:T(1024)S(1)} %get-tuple-element.8), kind=kOutput, calls=%fused_computation.4 | convolution fusion | flops 7268990976 | bytes 6316032 | tf_op jit(solution)/shard_map/nk,kr->nr/dot_general | solution.py:131
  273.1 0.0 copy-start
  273.1 3.8 select_reduce_fusion
  277.6 0.0 copy-start.1
  277.6 0.8 convert_subtract_fusion
  278.4 0.1 select_add_fusion.1.a_ref
  278.6 32.1 %shard_map.60 = f32[512,512]{1,0:T(8,128)S(1)} custom-call(f32[512,512]{1,0:T(8,128)S(1)} %select_add_fusion.1.a_ref), custom_call_target="tpu_custom_call" | custom-call | flops 1010106368 | bytes 2097152 | tf_op jit(solution)/shard_map/pallas_call | solution.py:113
  310.7 2.7 convolution_convert_fusion.2
  313.4 9.4 %fusion = f32[1536,512]{1,0:T(8,128)S(1)} fusion(bf16[1536,512]{1,0:T(8,128)(2,1)S(1)} %convolution_convert_fusion.2, s32[1536]{0:T(1024)S(1)} %get-tuple-element.11, s32[1536]{0:T(1024)S(1)} %get-tuple-element.9, s32[1536]{0:T(1024)S(1)} %get-tuple-element.10, s32[1536]{0:T(1024)S(1)} %get-tuple-element.8), kind=kOutput, calls=%fused_computation.3 | convolution fusion | flops 7268990976 | bytes 4743168 | tf_op jit(solution)/shard_map/nm,nr->mr/dot_general | solution.py:131
  322.8 7.7 %convolution_convert_fusion.1 = bf16[1536,512]{1,0:T(8,128)(2,1)S(1)} fusion(f32[1536,1536]{1,0:T(8,128)S(1)} %bitcast.45, f32[1536,512]{1,0:T(8,128)S(1)} %fusion), kind=kOutput, calls=%fused_computation.28 | convolution fusion | flops 7248543744 | bytes 14155776 | tf_op jit(solution)/shard_map/km,mr->kr/dot_general | solution.py:131
  330.6 1.9 pad_maximum_fusion
  332.5 4.8 %collective-permute-start.2 = (bf16[2,1536,512]{2,1,0:T(8,128)(2,1)}, bf16[2,1536,512]{2,1,0:T(8,128)(2,1)}, u32[]{:S(2)}, u32[]{:S(2)}) collective-permute-start(bf16[2,1536,512]{2,1,0:T(8,128)(2,1)} %pad_maximum_fusion), channel_id=1, source_target_pairs={{0,16},{1,17},{10,26},{11,27},{20,4},{21,5},{30,14},{31,15}} | collective-permute-start | bytes 9437192 | tf_op jit(solution)/shard_map/ppermute | solution.py:145
  337.3 33.4 %collective-permute-done.2 = bf16[2,1536,512]{2,1,0:T(8,128)(2,1)} collective-permute-done((bf16[2,1536,512]{2,1,0:T(8,128)(2,1)}, bf16[2,1536,512]{2,1,0:T(8,128)(2,1)}, u32[]{:S(2)}, u32[]{:S(2)}) %collective-permute-start.2) | collective-permute-done | bytes 3145760 | tf_op jit(solution)/shard_map/ppermute | solution.py:145
  370.7 2.1 broadcast_select_fusion
  372.8 3.0 collective-permute-start.3
  375.8 2.1 collective-permute-start
  377.9 20.5 %collective-permute-done = bf16[192,512]{1,0:T(8,128)(2,1)} collective-permute-done((bf16[192,512]{1,0:T(8,128)(2,1)S(1)}, bf16[192,512]{1,0:T(8,128)(2,1)}, u32[]{:S(2)}, u32[]{:S(2)}) %collective-permute-start) | collective-permute-done | bytes 196640 | tf_op jit(solution)/shard_map/ppermute | solution.py:200
  398.4 2.0 fusion.28
  400.4 2.2 broadcast_select_fusion.1
  402.6 9.3 %fusion.12 = bf16[2,1,1536,512]{2,3,0,1:T(8,128)(2,1)} fusion(bf16[2,1536,512]{2,1,0:T(8,128)(2,1)} %broadcast_select_fusion.1, s32[]{:T(128)S(6)} %select_n.93, bf16[1,1536,512]{2,1,0:T(8,128)(2,1)S(1)} %bitcast.43, bf16[1,1536,512]{2,1,0:T(8,128)(2,1)} %bitcast.6), kind=kOutput, calls=%fused_computation.20 | convolution fusion | flops 3228041216 | bytes 9437188 | tf_op jit(solution)/shard_map/ns,irs->inr/dot_general | solution.py:210
  411.9 4.6 %copy.11 = bf16[2,1,1536,512]{3,2,1,0:T(8,128)(2,1)} copy(bf16[2,1,1536,512]{2,3,0,1:T(8,128)(2,1)} %fusion.12) | data formatting | bytes 6291456
  (14 shorter events, 0.1 us)
Async XLA Ops:
  7.2 245.8 %all-gather.2.cloned.1.call-start = ((), (), s32[]{:S(2)}) async-start(), calls=%async_computation | async-start | bytes 3538944 | tf_op jit(solution)/shard_map/all_gather | solution.py:166
  273.1 3.8 copy-start
  277.6 33.0 %copy-start.1 = (f32[1536,512]{1,0:T(8,128)S(1)}, f32[1536,512]{1,0:T(8,128)}, u32[]{:S(2)}) copy-start(f32[1536,512]{1,0:T(8,128)} %copy-done) | copy-start | bytes 9437188
  310.7 12.1 %slice-start = ((s8[9437184]{0:T(1024)(128)(4,1)}), s8[4194304]{0:T(1024)(128)(4,1)S(1)}, s32[]{:S(2)}) async-start(s8[9437184]{0:T(1024)(128)(4,1)} %bitcast.44), calls=%async_computation.1 | async-start | bytes 8388608
  313.3 9.5 %slice-start.1 = ((s8[9437184]{0:T(1024)(128)(4,1)}), s8[4194304]{0:T(1024)(128)(4,1)S(1)}, s32[]{:S(2)}) async-start(s8[9437184]{0:T(1024)(128)(4,1)} %bitcast.44), calls=%async_computation.2 | async-start | bytes 8388608
  313.4 9.5 %slice-start.2 = ((s8[9437184]{0:T(1024)(128)(4,1)}), s8[1048576]{0:T(1024)(128)(4,1)S(1)}, s32[]{:S(2)}) async-start(s8[9437184]{0:T(1024)(128)(4,1)} %bitcast.44), calls=%async_computation.3 | async-start | bytes 2097152
  332.5 38.2 %collective-permute-start.2 = (bf16[2,1536,512]{2,1,0:T(8,128)(2,1)}, bf16[2,1536,512]{2,1,0:T(8,128)(2,1)}, u32[]{:S(2)}, u32[]{:S(2)}) collective-permute-start(bf16[2,1536,512]{2,1,0:T(8,128)(2,1)} %pad_maximum_fusion), channel_id=1, source_target_pairs={{0,16},{1,17},{10,26},{11,27},{20,4},{21,5},{30,14},{31,15}} | collective-permute-start | bytes 9437192 | tf_op jit(solution)/shard_map/ppermute | solution.py:145
  372.8 27.6 %collective-permute-start.3 = (bf16[2,1536,512]{2,1,0:T(8,128)(2,1)}, bf16[2,1536,512]{2,1,0:T(8,128)(2,1)}, u32[]{:S(2)}, u32[]{:S(2)}) collective-permute-start(bf16[2,1536,512]{2,1,0:T(8,128)(2,1)} %broadcast_select_fusion), channel_id=1, source_target_pairs={{0,8},{16,24},{1,9},{17,25},{10,2},{26,18},{11,3},{27,19},{4,12},{... | collective-permute-start | bytes 9437192 | tf_op jit(solution)/shard_map/ppermute | solution.py:145
  375.8 26.8 %collective-permute-start.1 = (bf16[1536,512]{1,0:T(8,128)(2,1)S(1)}, bf16[1536,512]{1,0:T(8,128)(2,1)}, u32[]{:S(2)}, u32[]{:S(2)}) collective-permute-start(bf16[1536,512]{1,0:T(8,128)(2,1)S(1)} %convolution_convert_fusion.1), channel_id=1, source_target_pairs={{0,1},{1,0},{2,3},{3,2},{4,5},{5,4},{6,7},{7,6},{8,9},{9,8},{10,11... | collective-permute-start | bytes 4718600 | tf_op jit(solution)/shard_map/ppermute | solution.py:199
  375.8 22.6 %collective-permute-start = (bf16[192,512]{1,0:T(8,128)(2,1)S(1)}, bf16[192,512]{1,0:T(8,128)(2,1)}, u32[]{:S(2)}, u32[]{:S(2)}) collective-permute-start(bf16[192,512]{1,0:T(8,128)(2,1)S(1)} %get-tuple-element.12), channel_id=1, source_target_pairs={{0,1},{1,0},{2,3},{3,2},{4,5},{5,4},{6,7},{7,6},{8,9},{9,8},{10,11... | collective-permute-start | bytes 589832 | tf_op jit(solution)/shard_map/ppermute | solution.py:200
Sparse Core Ops, SparseCore 0:
  10.2 74.7 all-gather.1
